TPU v7x, 32 devices: a whole 2x2x4 slice. The times are simulated.
32 devices in a mesh: dp: 4 (over y, core), expert: 8 (over z, x).
Axes of the slice: x: 2, y: 2, z: 4, core: 2. Of those that a mesh axis runs over, the one named last changes fastest.
Arguments:
- qkv: bfloat16 [32, 128, 6144], P(('dp', 'expert')), may hold values from -6 to 6
- resid: bfloat16 [32, 128, 2048], P(('dp', 'expert')), may hold values from -54 to 54
- lengths: int32 [32], P(('dp', 'expert')), may hold values from 32 to 128
- norm_gain: float32 [2048], replicated, may hold values from 0.25 to 1.75
- expert_ids: int32 [32, 128, 2], P(('dp', 'expert')), may hold values from 0 to 7, all different within a row; in each aligned block of 128 rows (0 to 127, 128 to 255, ..., all dimensions but the last counted through in order) at most 64 rows name the same one
- gate_vals: bfloat16 [32, 128, 2], P(('dp', 'expert')), may hold values from 0.099609375 to 1
- w_gate: bfloat16 [8, 768, 2048], P('expert', None, 'dp'), may hold values from -0.125 to 0.125
- w_up: bfloat16 [8, 768, 2048], P('expert', None, 'dp'), may hold values from -0.125 to 0.125
- w_down: bfloat16 [8, 768, 2048], P('expert', None, 'dp'), may hold values from -0.21875 to 0.21875
- cotangent: bfloat16 [32, 128, 2048], P(('dp', 'expert')), may hold values from -6 to 6
Outputs:
- mixture: bfloat16 [32, 128, 2048], P(('dp', 'expert'))
- grad_stream: float32 [32, 128, 2048], P(('dp', 'expert'))
- grad_gate: float32 [8, 768, 2048], P('expert', None, 'dp')
- grad_up: float32 [8, 768, 2048], P('expert', None, 'dp')
- grad_down: float32 [8, 768, 2048], P('expert', None, 'dp')
Inputs may be any that keep to these rules, and one draw needn't show every extreme that they name: `expert_ids`: among the 128 tokens of one device, no expert is named by more than 64 routes, a bound that some block reaches; the 2 ids of a token differ.
All inputs are finite; a program needn't handle non-finite values.
Results may differ from a plain program's by a relative error of at most 0.015.
Values may be sent and summed in bfloat16 or wider, within the bound.
A program may use at most 128 MiB of HBM per device.

v0:
```python
import functools
import math

import jax
import jax.numpy as jnp
from jax import lax
from jax.experimental import pallas as pl
from jax.experimental.pallas import tpu as pltpu
from jax.sharding import PartitionSpec as P

HEADS = 16
MESH = pl.DeviceIdType.MESH
F32 = jnp.float32
BF16 = jnp.bfloat16
NT = (((1,), (1,)), ((), ()))
NN = (((1,), (0,)), ((), ()))
LEN, QKV, ATT, COT, ROW, OUT, GRD = range(7)


def attend_block(queries, key_rows, value_rows, live_mask, head_size):
    scores = jnp.einsum(
        "sthc,uthc->thsu", queries, key_rows, preferred_element_type=jnp.float32
    ) / math.sqrt(head_size)
    count = queries.shape[0]
    self_pair = jnp.arange(count)[:, None] == jnp.arange(count)[None, :]
    allowed = jnp.transpose(live_mask)[:, None, None, :] | self_pair[None, None, :, :]
    masked = jnp.where(allowed, scores, -jnp.inf)
    highest = jnp.max(masked, axis=-1, keepdims=True)
    raised = jnp.exp(masked - highest)
    weights = (raised / jnp.sum(raised, axis=-1, keepdims=True)).astype(jnp.bfloat16)
    attended = jnp.einsum(
        "thsu,uthc->sthc", weights, value_rows, preferred_element_type=jnp.float32
    )
    attended = jnp.where(live_mask[:, :, None, None], attended, 0.0)
    return attended.astype(jnp.bfloat16)


def padded_rows(values):
    return jnp.concatenate([jnp.zeros((1,) + values.shape[1:], values.dtype), values], axis=0)


def plain_body(qkv, resid, lengths, norm_gain, expert_ids, gate_vals, w_gate, w_up, w_down, cotangent):
    series_here, step_count, triple = qkv.shape
    model_width = triple // 3
    head_size = model_width // HEADS
    experts_here = w_gate.shape[0]
    owners = lax.axis_size("expert")
    experts_all = experts_here * owners
    top_count = expert_ids.shape[2]
    tok_rows = series_here * step_count
    route_count = tok_rows * top_count
    capacity = 2 * route_count // experts_all
    slot_count = owners * capacity
    present = (jnp.arange(step_count)[None, :] < lengths[:, None]).astype(jnp.bfloat16)
    time_major, live_flags = (
        lax.all_to_all(qkv, "expert", split_axis=1, concat_axis=0, tiled=True),
        lax.all_to_all(present, "expert", split_axis=1, concat_axis=0, tiled=True),
    )
    group_size, time_count = live_flags.shape
    split_heads = time_major.reshape(group_size, time_count, 3, HEADS, head_size)
    attended = attend_block(
        split_heads[:, :, 0],
        split_heads[:, :, 1],
        split_heads[:, :, 2],
        live_flags > 0.5,
        head_size,
    )
    series_back = lax.all_to_all(
        attended.reshape(group_size, time_count, model_width),
        "expert",
        split_axis=0,
        concat_axis=1,
        tiled=True,
    )
    stream = resid.astype(jnp.float32) + series_back.astype(jnp.float32)
    inverse = 1.0 / jnp.sqrt(jnp.mean(stream * stream, axis=-1, keepdims=True) + 1e-05)
    normed = (stream * inverse * norm_gain).astype(jnp.bfloat16)
    route_ids = expert_ids.reshape(route_count)
    onehot = (route_ids[:, None] == jnp.arange(experts_all, dtype=jnp.int32)[None, :]).astype(
        jnp.int32
    )
    running = jnp.cumsum(onehot, axis=0, dtype=jnp.int32) - 1
    position = jnp.sum(running * onehot, axis=1, dtype=jnp.int32)
    slot_index = route_ids * capacity + position
    filled = (
        jnp.zeros((experts_all * capacity,), jnp.int32)
        .at[slot_index]
        .set(jnp.arange(1, route_count + 1, dtype=jnp.int32))
    )
    token_of = jnp.where(filled > 0, (filled - 1) // top_count + 1, 0)
    layout = (owners, experts_here, capacity, model_width)
    normed_send = padded_rows(normed.reshape(tok_rows, model_width))[token_of].reshape(layout)
    adjoint_send = padded_rows(cotangent.reshape(tok_rows, model_width))[token_of].reshape(layout)
    gate_send = padded_rows(gate_vals.reshape(route_count))[filled].reshape(
        owners, experts_here, capacity
    )
    gate_full, up_full, down_full = (
        lax.all_gather(w_gate, "dp", axis=2, tiled=True),
        lax.all_gather(w_up, "dp", axis=2, tiled=True),
        lax.all_gather(w_down, "dp", axis=2, tiled=True),
    )
    normed_recv = lax.all_to_all(normed_send, "expert", split_axis=0, concat_axis=2, tiled=True)
    x_rows = normed_recv.reshape(experts_here, slot_count, model_width)
    gate_pre = jnp.einsum("esd,efd->esf", x_rows, gate_full, preferred_element_type=jnp.float32)
    up_pre = jnp.einsum("esd,efd->esf", x_rows, up_full, preferred_element_type=jnp.float32)
    sigmoid_gate = jax.nn.sigmoid(gate_pre)
    hidden = (gate_pre * sigmoid_gate * up_pre).astype(jnp.bfloat16)
    expert_out = jnp.einsum(
        "esf,efd->esd", hidden, down_full, preferred_element_type=jnp.float32
    ).astype(jnp.bfloat16)
    back_shape = (1, experts_here, slot_count, model_width)
    out_home = lax.all_to_all(
        expert_out.reshape(back_shape), "expert", split_axis=2, concat_axis=0, tiled=True
    )
    adjoint_recv, gate_recv = (
        lax.all_to_all(adjoint_send, "expert", split_axis=0, concat_axis=2, tiled=True),
        lax.all_to_all(gate_send, "expert", split_axis=0, concat_axis=2, tiled=True),
    )
    adjoint_rows = adjoint_recv.reshape(experts_here, slot_count, model_width)
    gate_rows = gate_recv.reshape(experts_here, slot_count)
    grad_out = (
        gate_rows.astype(jnp.float32)[:, :, None] * adjoint_rows.astype(jnp.float32)
    ).astype(jnp.bfloat16)
    grad_hidden = jnp.einsum(
        "esd,efd->esf", grad_out, down_full, preferred_element_type=jnp.float32
    )
    grad_gate_pre = (
        grad_hidden * up_pre * sigmoid_gate * (1.0 + gate_pre * (1.0 - sigmoid_gate))
    ).astype(jnp.bfloat16)
    grad_up_pre = (grad_hidden * gate_pre * sigmoid_gate).astype(jnp.bfloat16)
    part_gate = jnp.einsum(
        "esf,esd->efd", grad_gate_pre, x_rows, preferred_element_type=jnp.float32
    )
    part_up = jnp.einsum("esf,esd->efd", grad_up_pre, x_rows, preferred_element_type=jnp.float32)
    part_down = jnp.einsum("esf,esd->efd", hidden, grad_out, preferred_element_type=jnp.float32)
    grad_gate, grad_up, grad_down = (
        lax.psum_scatter(
            part_gate.astype(jnp.bfloat16), "dp", scatter_dimension=2, tiled=True
        ).astype(jnp.float32),
        lax.psum_scatter(
            part_up.astype(jnp.bfloat16), "dp", scatter_dimension=2, tiled=True
        ).astype(jnp.float32),
        lax.psum_scatter(
            part_down.astype(jnp.bfloat16), "dp", scatter_dimension=2, tiled=True
        ).astype(jnp.float32),
    )
    grad_rows = jnp.einsum(
        "esf,efd->esd", grad_gate_pre, gate_full, preferred_element_type=jnp.float32
    )
    grad_rows = (
        grad_rows
        + jnp.einsum("esf,efd->esd", grad_up_pre, up_full, preferred_element_type=jnp.float32)
    ).astype(jnp.bfloat16)
    grad_home = lax.all_to_all(
        grad_rows.reshape(back_shape), "expert", split_axis=2, concat_axis=0, tiled=True
    )
    out_route = out_home.reshape(experts_all * capacity, model_width)[slot_index].reshape(
        tok_rows, top_count, model_width
    )
    grad_route = grad_home.reshape(experts_all * capacity, model_width)[slot_index].reshape(
        tok_rows, top_count, model_width
    )
    gates = gate_vals.reshape(tok_rows, top_count).astype(jnp.float32)
    mixture = jnp.sum(gates[:, :, None] * out_route.astype(jnp.float32), axis=1).astype(
        jnp.bfloat16
    )
    grad_normed = jnp.sum(grad_route.astype(jnp.float32), axis=1).reshape(
        series_here, step_count, model_width
    )
    scaled = norm_gain * grad_normed
    grad_stream = inverse * scaled - stream * inverse * inverse * inverse * jnp.mean(
        stream * scaled, axis=-1, keepdims=True
    )
    return (
        mixture.reshape(series_here, step_count, model_width),
        grad_stream,
        grad_gate,
        grad_up,
        grad_down,
    )


def dot(a, b, dims=NN):
    return lax.dot_general(a, b, dims, preferred_element_type=F32)


def layer_kernel(
    ne, nd, qkv, lens, resid, gain, meta, wg, wu, wd, cot,
    mixture, gstream, parts_in,
    len_in, qkv_in, att_out, att_in, normed, inv_rms, hit, hit_t, hit_gt,
    row_out, row_in, cot_out, cot_in, out_in, grd_in, w_all, gate, up, grad_h,
    hidden, hidden_t, ggp, ggp_t, gup, gup_t, parts_out,
    send, recv, w_send, w_recv, p_send, p_recv, local,
):
    me = lax.axis_index("expert")
    md = lax.axis_index("dp")
    steps, width = resid.shape
    ff, wcol = wg.shape
    tb = steps // ne
    slots = row_in.shape[0]
    cap = slots // ne
    head = width // HEADS

    def rows(block, size):
        return pl.ds(pl.multiple_of(block * size, size), size)

    def cols(block, size, base=0):
        return pl.ds(pl.multiple_of(base + block * size, 128), size)

    def remote(kind, src, dst, to, slot):
        return pltpu.make_async_remote_copy(
            src_ref=src, dst_ref=dst, send_sem=send.at[kind, to], recv_sem=recv.at[kind, slot],
            device_id={"expert": to}, device_id_type=MESH,
        )

    def ends(kind):
        if kind == LEN:
            return lens, len_in, None, tb
        if kind == QKV:
            return qkv, qkv_in, tb, tb
        if kind == ATT:
            return att_out, att_in, tb, tb
        if kind == COT:
            return cot_out, cot_in, cap, cap
        if kind == ROW:
            return row_out, row_in, cap, cap
        if kind == OUT:
            return row_out, out_in, cap, cap
        return cot_out, grd_in, cap, cap

    def copy_to(kind, to, slot):
        src, dst, from_rows, to_rows = ends(kind)
        part = src if from_rows is None else src.at[rows(to, from_rows)]
        return remote(kind, part, dst.at[rows(slot, to_rows)], to, slot)

    def own(kind):
        src, dst, from_rows, to_rows = ends(kind)
        part = src if from_rows is None else src.at[rows(me, from_rows)]
        return pltpu.make_async_copy(part, dst.at[rows(me, to_rows)], local.at[kind])

    def each(count, base, act):
        def step(i, carry):
            act(lax.rem(base + i, count))
            return carry

        lax.fori_loop(1, count, step, 0)

    def launch(kind):
        each(ne, me, lambda p: copy_to(kind, p, me).start())
        own(kind).start()

    def arrived(kind):
        each(ne, me, lambda p: copy_to(kind, p, p).wait_recv())
        own(kind).wait()

    def sent(kind):
        each(ne, me, lambda p: copy_to(kind, p, me).wait_send())

    shards = (wg, wu, wd)

    def weight_to(k, to, slot):
        return pltpu.make_async_remote_copy(
            src_ref=shards[k], dst_ref=w_all.at[k, slot], send_sem=w_send.at[k, to],
            recv_sem=w_recv.at[k, slot], device_id={"dp": to}, device_id_type=MESH,
        )

    def weight_own(k):
        return pltpu.make_async_copy(shards[k], w_all.at[k, md], local.at[7 + k])

    def part_to(k, to, slot):
        return pltpu.make_async_remote_copy(
            src_ref=parts_out.at[k, to], dst_ref=parts_in.at[k, slot], send_sem=p_send.at[k, to],
            recv_sem=p_recv.at[k, slot], device_id={"dp": to}, device_id_type=MESH,
        )

    def part_own(k):
        return pltpu.make_async_copy(parts_out.at[k, md], parts_in.at[k, md], local.at[10 + k])

    barrier = pltpu.get_barrier_semaphore()
    each(ne, me, lambda p: pl.semaphore_signal(
        barrier, inc=1, device_id={"expert": p}, device_id_type=MESH))
    each(nd, md, lambda p: pl.semaphore_signal(
        barrier, inc=1, device_id={"dp": p}, device_id_type=MESH))
    pl.semaphore_wait(barrier, ne + nd - 2)

    launch(LEN)
    launch(QKV)
    for k in range(3):
        each(nd, md, lambda p: weight_to(k, p, md).start())
        weight_own(k).start()

    top = max(16, ne)
    expert = lax.broadcasted_iota(jnp.int32, (top, steps), 0).astype(F32)
    first, second = meta[0:1, :], meta[1:2, :]
    named = jnp.where(expert == first, 1.0, 0.0) + jnp.where(expert == second, 1.0, 0.0)
    before = lax.broadcasted_iota(jnp.int32, (steps, steps), 0) < lax.broadcasted_iota(
        jnp.int32, (steps, steps), 1
    )
    place = dot(named.astype(BF16), jnp.where(before, 1.0, 0.0).astype(BF16))
    place = jnp.where(named > 0.5, place, -1.0)
    value = jnp.where(expert == first, meta[2:3, :], meta[3:4, :])
    slot = lax.broadcasted_iota(jnp.int32, (cap, steps), 0).astype(F32)
    per = max(1, 128 // cap)
    for e in range(0, ne, per):
        ones, weighted = [], []
        for i in range(e, e + per):
            same = place[i : i + 1, :] == slot
            ones.append(jnp.where(same, 1.0, 0.0))
            weighted.append(jnp.where(same, value[i : i + 1, :], 0.0))
        one = jnp.concatenate(ones, axis=0)
        scaled = jnp.concatenate(weighted, axis=0)
        span = slice(e * cap, (e + per) * cap)
        hit[span, :] = one.astype(BF16)
        hit_t[:, span] = one.T.astype(BF16)
        hit_gt[:, span] = scaled.T.astype(BF16)
        cot_out[span, :] = dot(scaled.astype(BF16), cot[...]).astype(BF16)

    arrived(LEN)
    arrived(QKV)
    row_len = len_in[...].astype(F32)
    col_len = row_len.T
    r_id = lax.broadcasted_iota(jnp.int32, (steps, steps), 0)
    c_id = lax.broadcasted_iota(jnp.int32, (steps, steps), 1)
    r_time, c_time = lax.rem(r_id, tb), lax.rem(c_id, tb)
    start = me * tb
    seen = ((c_time + start).astype(F32) < col_len) | (r_id == c_id)
    bias = jnp.where((r_time == c_time) & seen, 0.0, -jnp.inf)
    live = jnp.where((r_time + start).astype(F32) < row_len, 1.0, 0.0)

    def attend(h, carry):
        q = qkv_in[:, cols(h, head)]
        k = qkv_in[:, cols(h, head, width)]
        v = qkv_in[:, cols(h, head, 2 * width)]
        scores = dot(q, k, NT) / math.sqrt(head) + bias
        raised = jnp.exp(scores - jnp.max(scores, axis=1, keepdims=True))
        weights = (raised / jnp.sum(raised, axis=1, keepdims=True)).astype(BF16)
        att_out[:, cols(h, head)] = (dot(weights, v) * live).astype(BF16)
        return carry

    lax.fori_loop(0, HEADS, attend, 0)
    launch(ATT)
    launch(COT)
    arrived(ATT)

    def norm(i, carry):
        r = rows(i, 16)
        stream = resid[r, :].astype(F32) + att_in[r, :].astype(F32)
        mean = jnp.sum(stream * stream, axis=1, keepdims=True) / width
        inverse = 1.0 / jnp.sqrt(mean + 1e-05)
        inv_rms[r, :] = jnp.broadcast_to(inverse, (16, 128))
        normed[r, :] = (stream * inverse * gain[...]).astype(BF16)
        return carry

    lax.fori_loop(0, steps // 16, norm, 0)

    def dispatch(j, carry):
        c = cols(j, wcol)
        row_out[:, c] = dot(hit[...], normed[:, c]).astype(BF16)
        return carry

    lax.fori_loop(0, nd, dispatch, 0)
    launch(ROW)
    for k in range(3):
        each(nd, md, lambda p: weight_to(k, p, p).wait_recv())
        weight_own(k).wait()
    arrived(ROW)

    gate[...] = jnp.zeros_like(gate)
    up[...] = jnp.zeros_like(up)
    grad_h[...] = jnp.zeros_like(grad_h)

    def forward(j, carry):
        x = row_in[:, cols(j, wcol)]
        gate[...] += dot(x, w_all[0, j], NT)
        up[...] += dot(x, w_all[1, j], NT)
        return carry

    lax.fori_loop(0, nd, forward, 0)

    def activate(i, carry):
        r = rows(i, 128)
        g = gate[r, :]
        value = g * (1.0 / (1.0 + jnp.exp(-g))) * up[r, :]
        hidden[r, :] = value.astype(BF16)
        hidden_t[:, cols(i, 128)] = value.T.astype(BF16)
        return carry

    lax.fori_loop(0, slots // 128, activate, 0)
    sent(ROW)

    def project(j, carry):
        row_out[:, cols(j, wcol)] = dot(hidden[...], w_all[2, j]).astype(BF16)
        return carry

    lax.fori_loop(0, nd, project, 0)
    launch(OUT)

    arrived(COT)

    def backward(j, carry):
        grad_h[...] += dot(cot_in[:, cols(j, wcol)], w_all[2, j], NT)
        return carry

    lax.fori_loop(0, nd, backward, 0)

    def differentiate(i, carry):
        r = rows(i, 128)
        c = cols(i, 128)
        g = gate[r, :]
        gh = grad_h[r, :]
        s = 1.0 / (1.0 + jnp.exp(-g))
        dg = gh * up[r, :] * s * (1.0 + g * (1.0 - s))
        ggp[r, :] = dg.astype(BF16)
        ggp_t[:, c] = dg.T.astype(BF16)
        du = gh * g * s
        gup[r, :] = du.astype(BF16)
        gup_t[:, c] = du.T.astype(BF16)
        return carry

    lax.fori_loop(0, slots // 128, differentiate, 0)

    def weigh(j):
        x = row_in[:, cols(j, wcol)]
        y = cot_in[:, cols(j, wcol)]
        parts_out[0, j] = dot(ggp_t[...], x).astype(BF16)
        parts_out[1, j] = dot(gup_t[...], x).astype(BF16)
        parts_out[2, j] = dot(hidden_t[...], y).astype(BF16)

    def weigh_send(j):
        weigh(j)
        for k in range(3):
            part_to(k, j, md).start()

    each(nd, md, weigh_send)
    sent(COT)

    def pull(j, carry):
        c = cols(j, wcol)
        cot_out[:, c] = (dot(ggp[...], w_all[0, j]) + dot(gup[...], w_all[1, j])).astype(BF16)
        return carry

    lax.fori_loop(0, nd, pull, 0)
    launch(GRD)
    weigh(md)
    for k in range(3):
        part_own(k).start()

    arrived(OUT)

    def mix(j, carry):
        c = cols(j, wcol)
        mixture[:, c] = dot(hit_gt[...], out_in[:, c]).astype(BF16)
        return carry

    lax.fori_loop(0, nd, mix, 0)
    arrived(GRD)

    def home(j, carry):
        c = cols(j, wcol)
        gstream[:, c] = dot(hit_t[...], grd_in[:, c])
        return carry

    lax.fori_loop(0, nd, home, 0)

    def finish(i, carry):
        r = rows(i, 16)
        stream = resid[r, :].astype(F32) + att_in[r, :].astype(F32)
        inverse = inv_rms[r, 0:1]
        scaled = gain[...] * gstream[r, :]
        mean = jnp.sum(stream * scaled, axis=1, keepdims=True) / width
        gstream[r, :] = inverse * scaled - stream * (inverse * inverse * inverse * mean)
        return carry

    lax.fori_loop(0, steps // 16, finish, 0)

    for k in range(3):
        each(nd, md, lambda p: part_to(k, p, p).wait_recv())
        each(nd, md, lambda p: part_to(k, p, md).wait_send())
        part_own(k).wait()
        each(nd, md, lambda p: weight_to(k, p, md).wait_send())
    for kind in (LEN, QKV, ATT, OUT, GRD):
        sent(kind)


def body(qkv, resid, lengths, norm_gain, expert_ids, gate_vals, w_gate, w_up, w_down, cotangent):
    series, steps, triple = qkv.shape
    width = triple // 3
    ne, nd = lax.axis_size("expert"), lax.axis_size("dp")
    _, ff, wcol = w_gate.shape
    routes = steps * expert_ids.shape[2]
    cap = 2 * routes // ne
    slots = ne * cap
    tb = steps // ne
    fits = (
        series == 1 and w_gate.shape[0] == 1 and steps == 128 and tb % 16 == 0
        and cap % 16 == 0 and slots % 128 == 0 and wcol % 128 == 0 and expert_ids.shape[2] == 2
        and width // HEADS == 128
    )
    if not fits:
        return plain_body(
            qkv, resid, lengths, norm_gain, expert_ids, gate_vals, w_gate, w_up, w_down, cotangent
        )
    meta = jnp.concatenate([expert_ids[0].astype(F32), gate_vals[0].astype(F32)], axis=1).T
    lens = jnp.broadcast_to(lengths.astype(BF16)[:, None], (tb, 128))
    vmem = pl.BlockSpec(memory_space=pltpu.VMEM)
    hbm = pl.BlockSpec(memory_space=pl.ANY)
    dma = pltpu.SemaphoreType.DMA
    flops = 2 * slots * ff * width * 9
    mixture, gstream, parts = pl.pallas_call(
        functools.partial(layer_kernel, ne, nd),
        out_shape=(
            jax.ShapeDtypeStruct((steps, width), BF16),
            jax.ShapeDtypeStruct((steps, width), F32),
            jax.ShapeDtypeStruct((3, nd, ff, wcol), BF16),
        ),
        in_specs=[hbm, vmem, vmem, vmem, vmem, hbm, hbm, hbm, vmem],
        out_specs=(vmem, vmem, hbm),
        scratch_shapes=[
            pltpu.VMEM((ne * tb, 128), BF16),
            pltpu.VMEM((steps, triple), BF16),
            pltpu.VMEM((steps, width), BF16),
            pltpu.VMEM((steps, width), BF16),
            pltpu.VMEM((steps, width), BF16),
            pltpu.VMEM((steps, 128), F32),
            pltpu.VMEM((slots, steps), BF16),
            pltpu.VMEM((steps, slots), BF16),
            pltpu.VMEM((steps, slots), BF16),
            pltpu.VMEM((slots, width), BF16),
            pltpu.VMEM((slots, width), BF16),
            pltpu.VMEM((slots, width), BF16),
            pltpu.VMEM((slots, width), BF16),
            pltpu.VMEM((slots, width), BF16),
            pltpu.VMEM((slots, width), BF16),
            pltpu.VMEM((3, nd, ff, wcol), BF16),
            pltpu.VMEM((slots, ff), F32),
            pltpu.VMEM((slots, ff), F32),
            pltpu.VMEM((slots, ff), F32),
            pltpu.VMEM((slots, ff), BF16),
            pltpu.VMEM((ff, slots), BF16),
            pltpu.VMEM((slots, ff), BF16),
            pltpu.VMEM((ff, slots), BF16),
            pltpu.VMEM((slots, ff), BF16),
            pltpu.VMEM((ff, slots), BF16),
            pltpu.VMEM((3, nd, ff, wcol), BF16),
            dma((7, ne)),
            dma((7, ne)),
            dma((3, nd)),
            dma((3, nd)),
            dma((3, nd)),
            dma((3, nd)),
            dma((16,)),
        ],
        compiler_params=pltpu.CompilerParams(
            collective_id=0, has_side_effects=True, vmem_limit_bytes=60 * 1024 * 1024
        ),
        cost_estimate=pl.CostEstimate(
            flops=flops, bytes_accessed=30_000_000, transcendentals=2 * slots * ff
        ),
    )(
        qkv[0], lens, resid[0], norm_gain[None, :], meta, w_gate[0], w_up[0], w_down[0],
        cotangent[0],
    )
    grads = [jnp.sum(parts[k].astype(F32), axis=0)[None] for k in range(3)]
    return (mixture[None], gstream[None], *grads)


def solution(mesh):
    in_specs = (
        P(("dp", "expert"), None, None),
        P(("dp", "expert"), None, None),
        P(("dp", "expert")),
        P(),
        P(("dp", "expert"), None, None),
        P(("dp", "expert"), None, None),
        P("expert", None, "dp"),
        P("expert", None, "dp"),
        P("expert", None, "dp"),
        P(("dp", "expert"), None, None),
    )
    out_specs = (
        P(("dp", "expert"), None, None),
        P(("dp", "expert"), None, None),
        P("expert", None, "dp"),
        P("expert", None, "dp"),
        P("expert", None, "dp"),
    )
    return jax.shard_map(body, mesh=mesh, in_specs=in_specs, out_specs=out_specs, check_vma=False)
```

profile of v0, /device:TPU:26, one launch (start us, length us, event | category | flops | bytes accessed | tf_op | source)
XLA Modules:
  0.0 275.1 jit_solution(634654376975053828)
XLA Ops:
  1.3 0.7 convert_bitcast_fusion
  2.0 0.7 bitcast_convert_fusion
  2.6 0.6 maximum_bitcast_fusion.meta
  3.2 0.6 broadcast_in_dim.27.lens
  3.8 262.4 %shard_map.137 = (bf16[128,2048]{1,0:T(8,128)(2,1)}, f32[128,2048]{1,0:T(8,128)}, bf16[3,4,768,512]{3,2,1,0:T(8,128)(2,1)}) custom-call(bf16[128,6144]{1,0:T(8,128)(2,1)} %bitcast.25, bf16[16,128]{1,0:T(8,128)(2,1)} %broadcast_in_dim.27.lens, bf16[128,2048]{1,0:T(8,128)(2,1)} %bitcast.29, f32[1,2048]{1,0:T(1,128)} %bitcast.31, ...), custom_call_target="tpu_custom_call" | custom-call | flops 14495514624 | bytes 30000000 | tf_op jit(solution)/shard_map/pallas_call | solution.py:509
  266.2 0.0 copy-start.1
  266.2 0.0 copy-start
  266.2 7.2 %convert_reduce_fusion = (f32[768,512]{1,0:T(8,128)}, f32[768,512]{1,0:T(8,128)}, f32[768,512]{1,0:T(8,128)}) fusion(bf16[3,4,768,512]{3,2,1,0:T(8,128)(2,1)} %get-tuple-element.10), kind=kLoop, calls=%fused_computation | loop fusion | flops 8257536 | bytes 14155776 | tf_op jit(solution)/shard_map/reduce_sum | solution.py:563
  273.4 0.0 copy-done.1
  273.4 0.8 copy.18
  274.2 0.0 copy-done
  274.2 1.0 copy.19
Async XLA Ops:
  266.2 7.2 %copy-start.1 = (bf16[128,2048]{1,0:T(8,128)(2,1)S(1)}, bf16[128,2048]{1,0:T(8,128)(2,1)}, u32[]{:S(2)}) copy-start(bf16[128,2048]{1,0:T(8,128)(2,1)} %get-tuple-element.8) | copy-start | bytes 1572868
  266.2 8.0 %copy-start = (f32[128,2048]{1,0:T(8,128)S(1)}, f32[128,2048]{1,0:T(8,128)}, u32[]{:S(2)}) copy-start(f32[128,2048]{1,0:T(8,128)} %get-tuple-element.9) | copy-start | bytes 3145732
where the time goes:
time: 277 us; the launch traced here: 275 us
  Pallas kernels  262 us (95%)
  other arithmetic  9.1 us (3%)
    pallas_call x1, Pallas kernels, body(): pl.pallas_call(functools.partial(layer_kernel, ne, nd), out_shape=(jax.Sh...  262 us
    reduce_sum x1, other arithmetic, body(): grads = [jnp.sum(parts[k].astype(F32), axis=0)[None] for k in range(3)]  7.18 us

commit v1 on v0

--- a/solution.py
+++ b/solution.py
@@ -14,7 +14,7 @@
 BF16 = jnp.bfloat16
 NT = (((1,), (1,)), ((), ()))
 NN = (((1,), (0,)), ((), ()))
-LEN, QKV, ATT, COT, ROW, OUT, GRD = range(7)
+LEN, QKV, ATT, COT, ROW, OUT, GRD, COT2 = range(8)
 
 
 def attend_block(queries, key_rows, value_rows, live_mask, head_size):
@@ -186,16 +186,20 @@
 
 def layer_kernel(
     ne, nd, qkv, lens, resid, gain, meta, wg, wu, wd, cot,
-    mixture, gstream, parts_in,
+    mixture, gstream, g_gate, g_up, g_down,
     len_in, qkv_in, att_out, att_in, normed, inv_rms, hit, hit_t, hit_gt,
     row_out, row_in, cot_out, cot_in, out_in, grd_in, w_all, gate, up, grad_h,
-    hidden, hidden_t, ggp, ggp_t, gup, gup_t, parts_out,
-    send, recv, w_send, w_recv, p_send, p_recv, local,
+    hidden, hidden_t, ggp, ggp_t, gup, gup_t,
+    sib_out, sib_in, kept, far_in, total,
+    send, recv, w_send, w_recv, s_send, s_recv, f_send, f_recv, local,
 ):
     me = lax.axis_index("expert")
     md = lax.axis_index("dp")
     steps, width = resid.shape
     ff, wcol = wg.shape
+    sib = md + 1 - 2 * lax.rem(md, 2)
+    far = lax.rem(md + 2, nd)
+    diag = lax.rem(sib + 2, nd)
     tb = steps // ne
     slots = row_in.shape[0]
     cap = slots // ne
@@ -220,7 +224,7 @@
             return qkv, qkv_in, tb, tb
         if kind == ATT:
             return att_out, att_in, tb, tb
-        if kind == COT:
+        if kind in (COT, COT2):
             return cot_out, cot_in, cap, cap
         if kind == ROW:
             return row_out, row_in, cap, cap
@@ -228,15 +232,22 @@
             return row_out, out_in, cap, cap
         return cot_out, grd_in, cap, cap
 
+    def span(kind, block, size):
+        if kind == COT:
+            return rows(2 * block, size // 2)
+        if kind == COT2:
+            return rows(2 * block + 1, size // 2)
+        return rows(block, size)
+
     def copy_to(kind, to, slot):
         src, dst, from_rows, to_rows = ends(kind)
-        part = src if from_rows is None else src.at[rows(to, from_rows)]
-        return remote(kind, part, dst.at[rows(slot, to_rows)], to, slot)
+        part = src if from_rows is None else src.at[span(kind, to, from_rows)]
+        return remote(kind, part, dst.at[span(kind, slot, to_rows)], to, slot)
 
     def own(kind):
         src, dst, from_rows, to_rows = ends(kind)
-        part = src if from_rows is None else src.at[rows(me, from_rows)]
-        return pltpu.make_async_copy(part, dst.at[rows(me, to_rows)], local.at[kind])
+        part = src if from_rows is None else src.at[span(kind, me, from_rows)]
+        return pltpu.make_async_copy(part, dst.at[span(kind, me, to_rows)], local.at[kind])
 
     def each(count, base, act):
         def step(i, carry):
@@ -258,35 +269,44 @@
 
     shards = (wg, wu, wd)
 
-    def weight_to(k, to, slot):
+    def weight_to(k, way, slot):
+        src = w_all.at[k, slot] if way == 2 else shards[k]
         return pltpu.make_async_remote_copy(
-            src_ref=shards[k], dst_ref=w_all.at[k, slot], send_sem=w_send.at[k, to],
-            recv_sem=w_recv.at[k, slot], device_id={"dp": to}, device_id_type=MESH,
+            src_ref=src, dst_ref=w_all.at[k, slot], send_sem=w_send.at[k, way],
+            recv_sem=w_recv.at[k, slot], device_id={"dp": far if way == 1 else sib},
+            device_id_type=MESH,
         )
 
     def weight_own(k):
-        return pltpu.make_async_copy(shards[k], w_all.at[k, md], local.at[7 + k])
-
-    def part_to(k, to, slot):
+        return pltpu.make_async_copy(shards[k], w_all.at[k, md], local.at[8 + k])
+
+    def near_part(k, half):
         return pltpu.make_async_remote_copy(
-            src_ref=parts_out.at[k, to], dst_ref=parts_in.at[k, slot], send_sem=p_send.at[k, to],
-            recv_sem=p_recv.at[k, slot], device_id={"dp": to}, device_id_type=MESH,
+            src_ref=sib_out.at[k, half], dst_ref=sib_in.at[k, half], send_sem=s_send.at[k, half],
+            recv_sem=s_recv.at[k, half], device_id={"dp": sib}, device_id_type=MESH,
         )
 
-    def part_own(k):
-        return pltpu.make_async_copy(parts_out.at[k, md], parts_in.at[k, md], local.at[10 + k])
+    def far_part(k):
+        return pltpu.make_async_remote_copy(
+            src_ref=kept.at[k, 0], dst_ref=far_in.at[k], send_sem=f_send.at[k],
+            recv_sem=f_recv.at[k], device_id={"dp": far}, device_id_type=MESH,
+        )
+
+    def result(k):
+        return pltpu.make_async_copy(total.at[k], (g_gate, g_up, g_down)[k], local.at[11 + k])
 
     barrier = pltpu.get_barrier_semaphore()
     each(ne, me, lambda p: pl.semaphore_signal(
         barrier, inc=1, device_id={"expert": p}, device_id_type=MESH))
-    each(nd, md, lambda p: pl.semaphore_signal(
-        barrier, inc=1, device_id={"dp": p}, device_id_type=MESH))
-    pl.semaphore_wait(barrier, ne + nd - 2)
+    for p in (sib, far):
+        pl.semaphore_signal(barrier, inc=1, device_id={"dp": p}, device_id_type=MESH)
+    pl.semaphore_wait(barrier, ne + 1)
 
     launch(LEN)
     launch(QKV)
     for k in range(3):
-        each(nd, md, lambda p: weight_to(k, p, md).start())
+        weight_to(k, 1, md).start()
+        weight_to(k, 0, md).start()
         weight_own(k).start()
 
     top = max(16, ne)
@@ -309,14 +329,15 @@
             weighted.append(jnp.where(same, value[i : i + 1, :], 0.0))
         one = jnp.concatenate(ones, axis=0)
         scaled = jnp.concatenate(weighted, axis=0)
-        span = slice(e * cap, (e + per) * cap)
-        hit[span, :] = one.astype(BF16)
-        hit_t[:, span] = one.T.astype(BF16)
-        hit_gt[:, span] = scaled.T.astype(BF16)
-        cot_out[span, :] = dot(scaled.astype(BF16), cot[...]).astype(BF16)
+        piece = slice(e * cap, (e + per) * cap)
+        hit[piece, :] = one.astype(BF16)
+        hit_t[:, piece] = one.T.astype(BF16)
+        hit_gt[:, piece] = scaled.T.astype(BF16)
+        cot_out[piece, :] = dot(scaled.astype(BF16), cot[...]).astype(BF16)
 
     arrived(LEN)
     arrived(QKV)
+    launch(COT)
     row_len = len_in[...].astype(F32)
     col_len = row_len.T
     r_id = lax.broadcasted_iota(jnp.int32, (steps, steps), 0)
@@ -339,7 +360,6 @@
 
     lax.fori_loop(0, HEADS, attend, 0)
     launch(ATT)
-    launch(COT)
     arrived(ATT)
 
     def norm(i, carry):
@@ -361,7 +381,13 @@
     lax.fori_loop(0, nd, dispatch, 0)
     launch(ROW)
     for k in range(3):
-        each(nd, md, lambda p: weight_to(k, p, p).wait_recv())
+        weight_to(k, 1, far).wait_recv()
+        weight_to(k, 2, far).start()
+    sent(ROW)
+    launch(COT2)
+    for k in range(3):
+        weight_to(k, 0, sib).wait_recv()
+        weight_to(k, 2, diag).wait_recv()
         weight_own(k).wait()
     arrived(ROW)
 
@@ -386,7 +412,6 @@
         return carry
 
     lax.fori_loop(0, slots // 128, activate, 0)
-    sent(ROW)
 
     def project(j, carry):
         row_out[:, cols(j, wcol)] = dot(hidden[...], w_all[2, j]).astype(BF16)
@@ -396,6 +421,18 @@
     launch(OUT)
 
     arrived(COT)
+    arrived(COT2)
+    lefts, rights = (ggp_t, gup_t, hidden_t), (row_in, row_in, cot_in)
+
+    def part(k, j):
+        return dot(lefts[k][...], rights[k][:, cols(j, wcol)]).astype(BF16)
+
+    def both_parts(k, half):
+        sib_out[k, half] = part(k, sib if half else diag)
+        near_part(k, half).start()
+        kept[k, half] = part(k, md if half else far)
+
+    both_parts(2, 0)
 
     def backward(j, carry):
         grad_h[...] += dot(cot_in[:, cols(j, wcol)], w_all[2, j], NT)
@@ -419,20 +456,10 @@
 
     lax.fori_loop(0, slots // 128, differentiate, 0)
 
-    def weigh(j):
-        x = row_in[:, cols(j, wcol)]
-        y = cot_in[:, cols(j, wcol)]
-        parts_out[0, j] = dot(ggp_t[...], x).astype(BF16)
-        parts_out[1, j] = dot(gup_t[...], x).astype(BF16)
-        parts_out[2, j] = dot(hidden_t[...], y).astype(BF16)
-
-    def weigh_send(j):
-        weigh(j)
-        for k in range(3):
-            part_to(k, j, md).start()
-
-    each(nd, md, weigh_send)
+    both_parts(0, 0)
+    both_parts(1, 0)
     sent(COT)
+    sent(COT2)
 
     def pull(j, carry):
         c = cols(j, wcol)
@@ -441,9 +468,20 @@
 
     lax.fori_loop(0, nd, pull, 0)
     launch(GRD)
-    weigh(md)
-    for k in range(3):
-        part_own(k).start()
+    for k in (2, 0, 1):
+        near_part(k, 0).wait_recv()
+
+        def join(i, carry):
+            r = rows(i, 128)
+            kept[k, 0, r, :] = (
+                kept[k, 0, r, :].astype(F32) + sib_in[k, 0, r, :].astype(F32)
+            ).astype(BF16)
+            return carry
+
+        lax.fori_loop(0, ff // 128, join, 0)
+        far_part(k).start()
+    for k in (2, 0, 1):
+        both_parts(k, 1)
 
     arrived(OUT)
 
@@ -453,6 +491,19 @@
         return carry
 
     lax.fori_loop(0, nd, mix, 0)
+    for k in (2, 0, 1):
+        near_part(k, 1).wait_recv()
+        far_part(k).wait_recv()
+
+        def conclude(i, carry):
+            r = rows(i, 128)
+            total[k, r, :] = (
+                kept[k, 1, r, :].astype(F32) + sib_in[k, 1, r, :].astype(F32)
+            ) + far_in[k, r, :].astype(F32)
+            return carry
+
+        lax.fori_loop(0, ff // 128, conclude, 0)
+        result(k).start()
     arrived(GRD)
 
     def home(j, carry):
@@ -474,10 +525,13 @@
     lax.fori_loop(0, steps // 16, finish, 0)
 
     for k in range(3):
-        each(nd, md, lambda p: part_to(k, p, p).wait_recv())
-        each(nd, md, lambda p: part_to(k, p, md).wait_send())
-        part_own(k).wait()
-        each(nd, md, lambda p: weight_to(k, p, md).wait_send())
+        for half in range(2):
+            near_part(k, half).wait_send()
+        far_part(k).wait_send()
+        result(k).wait()
+        weight_to(k, 0, md).wait_send()
+        weight_to(k, 1, md).wait_send()
+        weight_to(k, 2, far).wait_send()
     for kind in (LEN, QKV, ATT, OUT, GRD):
         sent(kind)
 
@@ -492,7 +546,7 @@
     slots = ne * cap
     tb = steps // ne
     fits = (
-        series == 1 and w_gate.shape[0] == 1 and steps == 128 and tb % 16 == 0
+        nd == 4 and ff % 128 == 0 and cap % 32 == 0 and series == 1 and w_gate.shape[0] == 1 and steps == 128 and tb % 16 == 0
         and cap % 16 == 0 and slots % 128 == 0 and wcol % 128 == 0 and expert_ids.shape[2] == 2
         and width // HEADS == 128
     )
@@ -506,15 +560,15 @@
     hbm = pl.BlockSpec(memory_space=pl.ANY)
     dma = pltpu.SemaphoreType.DMA
     flops = 2 * slots * ff * width * 9
-    mixture, gstream, parts = pl.pallas_call(
+    mixture, gstream, *grads = pl.pallas_call(
         functools.partial(layer_kernel, ne, nd),
         out_shape=(
             jax.ShapeDtypeStruct((steps, width), BF16),
             jax.ShapeDtypeStruct((steps, width), F32),
-            jax.ShapeDtypeStruct((3, nd, ff, wcol), BF16),
+            *[jax.ShapeDtypeStruct((ff, wcol), F32) for _ in range(3)],
         ),
         in_specs=[hbm, vmem, vmem, vmem, vmem, hbm, hbm, hbm, vmem],
-        out_specs=(vmem, vmem, hbm),
+        out_specs=(vmem, vmem, hbm, hbm, hbm),
         scratch_shapes=[
             pltpu.VMEM((ne * tb, 128), BF16),
             pltpu.VMEM((steps, triple), BF16),
@@ -541,17 +595,23 @@
             pltpu.VMEM((ff, slots), BF16),
             pltpu.VMEM((slots, ff), BF16),
             pltpu.VMEM((ff, slots), BF16),
-            pltpu.VMEM((3, nd, ff, wcol), BF16),
-            dma((7, ne)),
-            dma((7, ne)),
+            pltpu.VMEM((3, 2, ff, wcol), BF16),
+            pltpu.VMEM((3, 2, ff, wcol), BF16),
+            pltpu.VMEM((3, 2, ff, wcol), BF16),
+            pltpu.VMEM((3, ff, wcol), BF16),
+            pltpu.VMEM((3, ff, wcol), F32),
+            dma((8, ne)),
+            dma((8, ne)),
+            dma((3, 3)),
             dma((3, nd)),
-            dma((3, nd)),
-            dma((3, nd)),
-            dma((3, nd)),
+            dma((3, 2)),
+            dma((3, 2)),
+            dma((3,)),
+            dma((3,)),
             dma((16,)),
         ],
         compiler_params=pltpu.CompilerParams(
-            collective_id=0, has_side_effects=True, vmem_limit_bytes=60 * 1024 * 1024
+            collective_id=0, has_side_effects=True, vmem_limit_bytes=62 * 1024 * 1024
         ),
         cost_estimate=pl.CostEstimate(
             flops=flops, bytes_accessed=30_000_000, transcendentals=2 * slots * ff
@@ -560,8 +620,7 @@
         qkv[0], lens, resid[0], norm_gain[None, :], meta, w_gate[0], w_up[0], w_down[0],
         cotangent[0],
     )
-    grads = [jnp.sum(parts[k].astype(F32), axis=0)[None] for k in range(3)]
-    return (mixture[None], gstream[None], *grads)
+    return (mixture[None], gstream[None], *[grad[None] for grad in grads])
 
 
 def solution(mesh):

time: 277 us -> 258 us (0.931)
  Pallas kernels: 262 us -> 245 us
  other arithmetic: 9.1 us -> 1.93 us
  local copies, waits for them, and re-layouts: 2.37 us -> 8.7 us
    pallas_call x1, Pallas kernels: 262 us -> 245 us  [body(): pl.pallas_call(functools.partial(layer_kernel, ne, nd), out_shape=(jax.Sh...]
    reduce_sum x1 -> x0, other arithmetic: 7.18 us -> none  [body(): grads = [jnp.sum(parts[k].astype(F32), axis=0)[None] for k in range(3)]]
    unnamed x6 -> x13, local copies, waits for them, and re-layouts: 1.77 us -> 8.1 us
where the time goes in v1:
time: 258 us; the launch traced here: 257 us
  Pallas kernels  245 us (95%)
  local copies, waits for them, and re-layouts  8.7 us (3%)
    pallas_call x1, Pallas kernels, body(): pl.pallas_call(functools.partial(layer_kernel, ne, nd), out_shape=(jax.Sh...  245 us
    unnamed x13, local copies, waits for them, and re-layouts  8.1 us

profile of v1, /device:TPU:26, one launch (start us, length us, event | category | flops | bytes accessed | tf_op | source)
XLA Modules:
  0.0 257.4 jit_solution(4690797896898494499)
XLA Ops:
  1.3 0.7 convert_bitcast_fusion
  2.0 0.7 bitcast_convert_fusion
  2.6 0.6 maximum_bitcast_fusion.meta
  3.2 0.6 broadcast_in_dim.27.lens
  3.8 245.5 %shard_map.137 = (bf16[128,2048]{1,0:T(8,128)(2,1)}, f32[128,2048]{1,0:T(8,128)}, f32[768,512]{1,0:T(8,128)}, f32[768,512]{1,0:T(8,128)}, f32[768,512]{1,0:T(8,128)}) custom-call(bf16[128,6144]{1,0:T(8,128)(2,1)} %bitcast.25, bf16[16,128]{1,0:T(8,128)(2,1)} %broadcast_in_dim.27.lens, bf16[128,2048]{1,0:T(8,128)(2,1)} %bitcast.29, f32[1,2048]{1,0:T(1,128)} %bitcast.31, ...), custom_call_target="tpu_custom_call" | custom-call | flops 14495514624 | bytes 30000000 | tf_op jit(solution)/shard_map/pallas_call | solution.py:563
  249.3 0.0 copy-start.3
  249.3 0.0 copy-start.2
  249.3 2.0 copy.21
  251.3 0.0 copy-done.3
  251.3 1.0 copy.22
  252.3 0.0 copy-done.2
  252.3 0.0 copy-start.1
  252.3 1.1 copy.23
  253.5 0.8 copy-done.1
  254.3 0.0 copy-start
  254.3 1.1 copy.24
  255.4 0.8 copy-done
  256.3 1.1 copy.25
Async XLA Ops:
  249.3 2.1 copy-start.3
  249.3 3.0 %copy-start.2 = (f32[768,512]{1,0:T(8,128)S(1)}, f32[768,512]{1,0:T(8,128)}, u32[]{:S(2)}) copy-start(f32[768,512]{1,0:T(8,128)} %get-tuple-element.12) | copy-start | bytes 4718596
  252.3 2.0 copy-start.1
  254.3 2.0 copy-start

commit v2 on v1

--- a/solution.py
+++ b/solution.py
@@ -14,7 +14,7 @@
 BF16 = jnp.bfloat16
 NT = (((1,), (1,)), ((), ()))
 NN = (((1,), (0,)), ((), ()))
-LEN, QKV, ATT, COT, ROW, OUT, GRD, COT2 = range(8)
+LEN, QKV, ATT, COT, ROW, OUT, GRD, INFO = range(8)
 
 
 def attend_block(queries, key_rows, value_rows, live_mask, head_size):
@@ -185,9 +185,10 @@
 
 
 def layer_kernel(
-    ne, nd, qkv, lens, resid, gain, meta, wg, wu, wd, cot,
+    ne, nd, qkv, lens, resid, gain, info, wg, wu, wd, cot,
     mixture, gstream, g_gate, g_up, g_down,
-    len_in, qkv_in, att_out, att_in, normed, inv_rms, hit, hit_t, hit_gt,
+    len_in, qkv_in, att_out, att_in, normed, inv_rms, hit, hit_g, hit_t, hit_gt,
+    far_info, far_hit, far_hit_g, far_rows, far_cot,
     row_out, row_in, cot_out, cot_in, out_in, grd_in, w_all, gate, up, grad_h,
     hidden, hidden_t, ggp, ggp_t, gup, gup_t,
     sib_out, sib_in, kept, far_in, total,
@@ -200,6 +201,10 @@
     sib = md + 1 - 2 * lax.rem(md, 2)
     far = lax.rem(md + 2, nd)
     diag = lax.rem(sib + 2, nd)
+    half = ne // 2
+    base = lax.div(me, half) * half
+    other = half - base
+    mate = me - base + other
     tb = steps // ne
     slots = row_in.shape[0]
     cap = slots // ne
@@ -224,7 +229,7 @@
             return qkv, qkv_in, tb, tb
         if kind == ATT:
             return att_out, att_in, tb, tb
-        if kind in (COT, COT2):
+        if kind == COT:
             return cot_out, cot_in, cap, cap
         if kind == ROW:
             return row_out, row_in, cap, cap
@@ -232,22 +237,15 @@
             return row_out, out_in, cap, cap
         return cot_out, grd_in, cap, cap
 
-    def span(kind, block, size):
-        if kind == COT:
-            return rows(2 * block, size // 2)
-        if kind == COT2:
-            return rows(2 * block + 1, size // 2)
-        return rows(block, size)
-
     def copy_to(kind, to, slot):
         src, dst, from_rows, to_rows = ends(kind)
-        part = src if from_rows is None else src.at[span(kind, to, from_rows)]
-        return remote(kind, part, dst.at[span(kind, slot, to_rows)], to, slot)
+        part = src if from_rows is None else src.at[rows(to, from_rows)]
+        return remote(kind, part, dst.at[rows(slot, to_rows)], to, slot)
 
     def own(kind):
         src, dst, from_rows, to_rows = ends(kind)
-        part = src if from_rows is None else src.at[span(kind, me, from_rows)]
-        return pltpu.make_async_copy(part, dst.at[span(kind, me, to_rows)], local.at[kind])
+        part = src if from_rows is None else src.at[rows(me, from_rows)]
+        return pltpu.make_async_copy(part, dst.at[rows(me, to_rows)], local.at[kind])
 
     def each(count, base, act):
         def step(i, carry):
@@ -256,16 +254,75 @@
 
         lax.fori_loop(1, count, step, 0)
 
+    def all_peers(act):
+        def step(i, carry):
+            d = ne - i
+            side = lax.rem(lax.div(me, 4) + lax.div(d, 4), 2)
+            line = lax.rem(lax.rem(lax.div(me, 2), 2) + lax.rem(lax.div(d, 2), 2), 2)
+            edge = lax.rem(lax.rem(me, 2) + lax.rem(d, 2), 2)
+            act(4 * side + 2 * line + edge)
+            return carry
+
+        lax.fori_loop(1, ne, step, 0)
+
+    def near_peers(act):
+        def step(i, carry):
+            act(base + lax.rem(me - base + i, half))
+            return carry
+
+        lax.fori_loop(1, half, step, 0)
+
+    def across(kind):
+        src, dst = {INFO: (info, far_info), ROW: (normed, far_rows), COT: (cot, far_cot)}[kind]
+        return remote(kind, src, dst, mate, me)
+
+    def crossed(kind):
+        src, dst = {INFO: (info, far_info), ROW: (normed, far_rows), COT: (cot, far_cot)}[kind]
+        remote(kind, src, dst, mate, mate).wait_recv()
+
+    def relay(kind, p, slot):
+        src, dst, size, _ = ends(kind)
+        return pltpu.make_async_remote_copy(
+            src_ref=src.at[rows(p - base + other, size)], dst_ref=dst.at[rows(slot, size)],
+            send_sem=send.at[kind, p - base + other], recv_sem=recv.at[kind, slot],
+            device_id={"expert": p}, device_id_type=MESH,
+        )
+
+    def relay_own(kind):
+        src, dst, size, _ = ends(kind)
+        return pltpu.make_async_copy(
+            src.at[rows(mate, size)], dst.at[rows(mate, size)], local.at[kind + 11]
+        )
+
+    def launch_near(kind):
+        near_peers(lambda p: copy_to(kind, p, me).start())
+        own(kind).start()
+
+    def launch_relay(kind):
+        near_peers(lambda p: relay(kind, p, mate).start())
+        relay_own(kind).start()
+
+    def gathered(kind):
+        near_peers(lambda p: copy_to(kind, p, p).wait_recv())
+        near_peers(lambda p: relay(kind, p, p - base + other).wait_recv())
+        own(kind).wait()
+        relay_own(kind).wait()
+
+    def passed(kind):
+        near_peers(lambda p: copy_to(kind, p, me).wait_send())
+        near_peers(lambda p: relay(kind, p, mate).wait_send())
+        across(kind).wait_send()
+
     def launch(kind):
-        each(ne, me, lambda p: copy_to(kind, p, me).start())
+        all_peers(lambda p: copy_to(kind, p, me).start())
         own(kind).start()
 
     def arrived(kind):
-        each(ne, me, lambda p: copy_to(kind, p, p).wait_recv())
+        all_peers(lambda p: copy_to(kind, p, p).wait_recv())
         own(kind).wait()
 
     def sent(kind):
-        each(ne, me, lambda p: copy_to(kind, p, me).wait_send())
+        all_peers(lambda p: copy_to(kind, p, me).wait_send())
 
     shards = (wg, wu, wd)
 
@@ -293,7 +350,7 @@
         )
 
     def result(k):
-        return pltpu.make_async_copy(total.at[k], (g_gate, g_up, g_down)[k], local.at[11 + k])
+        return pltpu.make_async_copy(total.at[k], (g_gate, g_up, g_down)[k], local.at[18 + k])
 
     barrier = pltpu.get_barrier_semaphore()
     each(ne, me, lambda p: pl.semaphore_signal(
@@ -302,6 +359,7 @@
         pl.semaphore_signal(barrier, inc=1, device_id={"dp": p}, device_id_type=MESH)
     pl.semaphore_wait(barrier, ne + 1)
 
+    across(INFO).start()
     launch(LEN)
     launch(QKV)
     for k in range(3):
@@ -309,35 +367,60 @@
         weight_to(k, 0, md).start()
         weight_own(k).start()
 
-    top = max(16, ne)
-    expert = lax.broadcasted_iota(jnp.int32, (top, steps), 0).astype(F32)
-    first, second = meta[0:1, :], meta[1:2, :]
-    named = jnp.where(expert == first, 1.0, 0.0) + jnp.where(expert == second, 1.0, 0.0)
-    before = lax.broadcasted_iota(jnp.int32, (steps, steps), 0) < lax.broadcasted_iota(
-        jnp.int32, (steps, steps), 1
-    )
-    place = dot(named.astype(BF16), jnp.where(before, 1.0, 0.0).astype(BF16))
-    place = jnp.where(named > 0.5, place, -1.0)
-    value = jnp.where(expert == first, meta[2:3, :], meta[3:4, :])
+    row_id = lax.broadcasted_iota(jnp.int32, (steps, steps), 0)
+    col_id = lax.broadcasted_iota(jnp.int32, (steps, steps), 1)
+    before = jnp.where(row_id < col_id, 1.0, 0.0).astype(BF16)
     slot = lax.broadcasted_iota(jnp.int32, (cap, steps), 0).astype(F32)
-    per = max(1, 128 // cap)
-    for e in range(0, ne, per):
-        ones, weighted = [], []
-        for i in range(e, e + per):
-            same = place[i : i + 1, :] == slot
-            ones.append(jnp.where(same, 1.0, 0.0))
-            weighted.append(jnp.where(same, value[i : i + 1, :], 0.0))
-        one = jnp.concatenate(ones, axis=0)
-        scaled = jnp.concatenate(weighted, axis=0)
-        piece = slice(e * cap, (e + per) * cap)
+    per = 128 // cap
+
+    def routing(named_by, lowest, count, store):
+        known = named_by[...].astype(F32)
+        expert = (lax.broadcasted_iota(jnp.int32, (16, steps), 0) + lowest).astype(F32)
+        first, second = known[0:1, :], known[1:2, :]
+        named = jnp.where(expert == first, 1.0, 0.0) + jnp.where(expert == second, 1.0, 0.0)
+        place = jnp.where(named > 0.5, dot(named.astype(BF16), before), -1.0)
+        value = jnp.where(expert == first, known[2:3, :], known[3:4, :])
+        for e in range(0, count, per):
+            ones, weighted = [], []
+            for i in range(e, e + per):
+                same = place[i : i + 1, :] == slot
+                ones.append(jnp.where(same, 1.0, 0.0))
+                weighted.append(jnp.where(same, value[i : i + 1, :], 0.0))
+            store(
+                slice(e * cap, (e + per) * cap),
+                jnp.concatenate(ones, axis=0),
+                jnp.concatenate(weighted, axis=0),
+            )
+
+    def store_own(piece, one, scaled):
         hit[piece, :] = one.astype(BF16)
+        hit_g[piece, :] = scaled.astype(BF16)
         hit_t[:, piece] = one.T.astype(BF16)
         hit_gt[:, piece] = scaled.T.astype(BF16)
-        cot_out[piece, :] = dot(scaled.astype(BF16), cot[...]).astype(BF16)
+
+    def store_far(piece, one, scaled):
+        far_hit[piece, :] = one.astype(BF16)
+        far_hit_g[piece, :] = scaled.astype(BF16)
+
+    mine = pl.ds(pl.multiple_of(base * cap, half * cap), half * cap)
+    theirs = pl.ds(pl.multiple_of(other * cap, half * cap), half * cap)
+
+    def cut(where, choose, source, target):
+        def step(j, carry):
+            c = cols(j, wcol)
+            target[where, c] = dot(choose, source[:, c]).astype(BF16)
+            return carry
+
+        lax.fori_loop(0, nd, step, 0)
+
+    routing(info, 0, ne, store_own)
+    crossed(INFO)
+    routing(far_info, base, half, store_far)
+    cut(mine, hit_g[mine, :], cot, cot_out)
 
     arrived(LEN)
     arrived(QKV)
-    launch(COT)
+    across(COT).start()
     row_len = len_in[...].astype(F32)
     col_len = row_len.T
     r_id = lax.broadcasted_iota(jnp.int32, (steps, steps), 0)
@@ -373,23 +456,24 @@
 
     lax.fori_loop(0, steps // 16, norm, 0)
 
-    def dispatch(j, carry):
-        c = cols(j, wcol)
-        row_out[:, c] = dot(hit[...], normed[:, c]).astype(BF16)
-        return carry
-
-    lax.fori_loop(0, nd, dispatch, 0)
-    launch(ROW)
+    across(ROW).start()
+    cut(mine, hit[mine, :], normed, row_out)
+    launch_near(ROW)
+    crossed(COT)
+    cut(theirs, far_hit_g[...], far_cot, cot_out)
+    crossed(ROW)
+    cut(theirs, far_hit[...], far_rows, row_out)
+    launch_relay(ROW)
+    launch_relay(COT)
+    launch_near(COT)
     for k in range(3):
         weight_to(k, 1, far).wait_recv()
         weight_to(k, 2, far).start()
-    sent(ROW)
-    launch(COT2)
     for k in range(3):
         weight_to(k, 0, sib).wait_recv()
         weight_to(k, 2, diag).wait_recv()
         weight_own(k).wait()
-    arrived(ROW)
+    gathered(ROW)
 
     gate[...] = jnp.zeros_like(gate)
     up[...] = jnp.zeros_like(up)
@@ -413,6 +497,8 @@
 
     lax.fori_loop(0, slots // 128, activate, 0)
 
+    passed(ROW)
+
     def project(j, carry):
         row_out[:, cols(j, wcol)] = dot(hidden[...], w_all[2, j]).astype(BF16)
         return carry
@@ -420,8 +506,7 @@
     lax.fori_loop(0, nd, project, 0)
     launch(OUT)
 
-    arrived(COT)
-    arrived(COT2)
+    gathered(COT)
     lefts, rights = (ggp_t, gup_t, hidden_t), (row_in, row_in, cot_in)
 
     def part(k, j):
@@ -458,8 +543,7 @@
 
     both_parts(0, 0)
     both_parts(1, 0)
-    sent(COT)
-    sent(COT2)
+    passed(COT)
 
     def pull(j, carry):
         c = cols(j, wcol)
@@ -534,6 +618,7 @@
         weight_to(k, 2, far).wait_send()
     for kind in (LEN, QKV, ATT, OUT, GRD):
         sent(kind)
+    across(INFO).wait_send()
 
 
 def body(qkv, resid, lengths, norm_gain, expert_ids, gate_vals, w_gate, w_up, w_down, cotangent):
@@ -546,7 +631,7 @@
     slots = ne * cap
     tb = steps // ne
     fits = (
-        nd == 4 and ff % 128 == 0 and cap % 32 == 0 and series == 1 and w_gate.shape[0] == 1 and steps == 128 and tb % 16 == 0
+        nd == 4 and ne == 8 and ff % 128 == 0 and cap % 32 == 0 and series == 1 and w_gate.shape[0] == 1 and steps == 128 and tb % 16 == 0
         and cap % 16 == 0 and slots % 128 == 0 and wcol % 128 == 0 and expert_ids.shape[2] == 2
         and width // HEADS == 128
     )
@@ -554,7 +639,8 @@
         return plain_body(
             qkv, resid, lengths, norm_gain, expert_ids, gate_vals, w_gate, w_up, w_down, cotangent
         )
-    meta = jnp.concatenate([expert_ids[0].astype(F32), gate_vals[0].astype(F32)], axis=1).T
+    routed = jnp.concatenate([expert_ids[0].astype(BF16), gate_vals[0]], axis=1)
+    info = jnp.pad(routed, ((0, 0), (0, 12))).T
     lens = jnp.broadcast_to(lengths.astype(BF16)[:, None], (tb, 128))
     vmem = pl.BlockSpec(memory_space=pltpu.VMEM)
     hbm = pl.BlockSpec(memory_space=pl.ANY)
@@ -577,8 +663,14 @@
             pltpu.VMEM((steps, width), BF16),
             pltpu.VMEM((steps, 128), F32),
             pltpu.VMEM((slots, steps), BF16),
+            pltpu.VMEM((slots, steps), BF16),
             pltpu.VMEM((steps, slots), BF16),
             pltpu.VMEM((steps, slots), BF16),
+            pltpu.VMEM((16, steps), BF16),
+            pltpu.VMEM((slots // 2, steps), BF16),
+            pltpu.VMEM((slots // 2, steps), BF16),
+            pltpu.VMEM((steps, width), BF16),
+            pltpu.VMEM((steps, width), BF16),
             pltpu.VMEM((slots, width), BF16),
             pltpu.VMEM((slots, width), BF16),
             pltpu.VMEM((slots, width), BF16),
@@ -608,7 +700,7 @@
             dma((3, 2)),
             dma((3,)),
             dma((3,)),
-            dma((16,)),
+            dma((24,)),
         ],
         compiler_params=pltpu.CompilerParams(
             collective_id=0, has_side_effects=True, vmem_limit_bytes=62 * 1024 * 1024
@@ -617,7 +709,7 @@
             flops=flops, bytes_accessed=30_000_000, transcendentals=2 * slots * ff
         ),
     )(
-        qkv[0], lens, resid[0], norm_gain[None, :], meta, w_gate[0], w_up[0], w_down[0],
+        qkv[0], lens, resid[0], norm_gain[None, :], info, w_gate[0], w_up[0], w_down[0],
         cotangent[0],
     )
     return (mixture[None], gstream[None], *[grad[None] for grad in grads])

time: 258 us -> 239 us (0.926); the launches traced: 257 us -> 235 us
  Pallas kernels: 245 us -> 223 us
    pallas_call x1, Pallas kernels: 245 us -> 223 us  [body(): pl.pallas_call(functools.partial(layer_kernel, ne, nd), out_shape=(jax.Sh...]
where the time goes in v2:
time: 239 us; the launch traced here: 235 us
  Pallas kernels  223 us (93%)
  local copies, waits for them, and re-layouts  8.7 us (4%)
    pallas_call x1, Pallas kernels, body(): pl.pallas_call(functools.partial(layer_kernel, ne, nd), out_shape=(jax.Sh...  223 us
    unnamed x13, local copies, waits for them, and re-layouts  8.1 us

profile of v2, /device:TPU:26, one launch (start us, length us, event | category | flops | bytes accessed | tf_op | source)
XLA Modules:
  0.0 234.6 jit_solution(6631024887075647788)
XLA Ops:
  1.3 0.7 convert_bitcast_fusion
  2.0 1.3 fusion.3.info
  3.2 0.6 broadcast_in_dim.27.lens
  3.8 222.7 %shard_map.137 = (bf16[128,2048]{1,0:T(8,128)(2,1)}, f32[128,2048]{1,0:T(8,128)}, f32[768,512]{1,0:T(8,128)}, f32[768,512]{1,0:T(8,128)}, f32[768,512]{1,0:T(8,128)}) custom-call(bf16[128,6144]{1,0:T(8,128)(2,1)} %bitcast.24, bf16[16,128]{1,0:T(8,128)(2,1)} %broadcast_in_dim.27.lens, bf16[128,2048]{1,0:T(8,128)(2,1)} %bitcast.28, f32[1,2048]{1,0:T(1,128)} %bitcast.30, ...), custom_call_target="tpu_custom_call" | custom-call | flops 14495514624 | bytes 30000000 | tf_op jit(solution)/shard_map/pallas_call | solution.py:649
  226.5 0.0 copy-start.3
  226.5 0.0 copy-start.2
  226.5 2.0 copy.21
  228.5 0.0 copy-done.3
  228.5 1.0 copy.22
  229.5 0.0 copy-done.2
  229.5 0.0 copy-start.1
  229.5 1.1 copy.23
  230.7 0.8 copy-done.1
  231.5 0.0 copy-start
  231.5 1.1 copy.24
  232.6 0.8 copy-done
  233.5 1.1 copy.25
Async XLA Ops:
  226.5 2.1 copy-start.3
  226.5 3.0 %copy-start.2 = (f32[768,512]{1,0:T(8,128)S(1)}, f32[768,512]{1,0:T(8,128)}, u32[]{:S(2)}) copy-start(f32[768,512]{1,0:T(8,128)} %get-tuple-element.12) | copy-start | bytes 4718596
  229.5 2.0 copy-start.1
  231.5 2.0 copy-start
